TPU v7x, 256 devices: a whole 4x4x8 slice. The times are simulated.
256 devices in a mesh: seq: 64 (over z, y, core), head: 4 (over x).
Axes of the slice: x: 4, y: 4, z: 8, core: 2. Of those that a mesh axis runs over, the one named last changes fastest.
Arguments:
- query_rows: bfloat16 [16384, 4096], P(('seq', 'head')), may hold values from -6 to 6
- key_rows: bfloat16 [16384, 4096], P(('seq', 'head')), may hold values from -6 to 6
- value_rows: bfloat16 [16384, 4096], P(('seq', 'head')), may hold values from -6 to 6
- log_decay: float32 [32, 16384], P('head', 'seq'), may hold values from -1 to 0, as said below
- regularizer: float32 [32], P('head'), may hold values from 0.25 to 2
- norm_gain: float32 [32, 128], P('head'), may hold values from 0.1 to 1.9
- out_weight: bfloat16 [4096, 4096], P('head'), may hold values from -0.09375 to 0.09375
Outputs:
- layer_output: bfloat16 [16384, 4096], P(('seq', 'head'))
Inputs may be any that keep to these rules, and one draw needn't show every extreme that they name: `log_decay`: each entry is the logarithm of a forget factor of one head at one token.
All inputs are finite; a program needn't handle non-finite values.
Results may differ from a plain program's by a relative error of at most 0.015.
Values may be sent and summed in bfloat16 or wider, within the bound.
A program may use at most 256 MiB of HBM per device.

v0:
```python
import jax
import jax.numpy as jnp
from jax import lax
from jax.sharding import PartitionSpec as P

SPAN = 128
ITERS = 4


HIGHEST = lax.Precision.HIGHEST
EPSILON = 1e-06


def prefix(shard, axis, combine, identity):
    devices, place = (lax.axis_size(axis), lax.axis_index(axis))
    everything = jax.tree.map(lambda part: lax.all_gather(part, axis), shard)
    start = jax.tree.map(
        lambda part, zero: jnp.broadcast_to(jnp.asarray(zero, part.dtype), part.shape),
        shard,
        identity,
    )

    def step(k, before):
        reached = k < place
        new = combine(before, jax.tree.map(lambda part: part[k], everything))
        return jax.tree.map(lambda a, b: jnp.where(reached, a, b), new, before)

    return lax.fori_loop(0, devices, step, start)


def unit_keys(unscaled):
    head_width = unscaled.shape[-1]
    return (
        unscaled
        * lax.rsqrt(jnp.mean(unscaled * unscaled, axis=-1, keepdims=True) + EPSILON)
        * head_width ** (-0.5)
    )


def causal_weights(cumulative):
    length = cumulative.shape[-1]
    spread = cumulative[..., :, None] - cumulative[..., None, :]
    causal_mask = jnp.arange(length)[:, None] >= jnp.arange(length)[None, :]
    return jnp.where(causal_mask, jnp.exp(jnp.minimum(spread, 0.0)), 0.0)


def to_blocks(flattened, heads_here):
    row_total = flattened.shape[0]
    head_width = flattened.shape[1] // heads_here
    shaped = flattened.astype(jnp.float32).reshape(row_total // SPAN, SPAN, heads_here, head_width)
    return jnp.transpose(shaped, (2, 0, 1, 3))


def solve_block(queries, normed_keys, values, cumulative, weights, gram_state, memory, ridge):
    carried = jnp.exp(cumulative)[..., None]
    ridge_term = ridge.reshape(ridge.shape + (1,) * (queries.ndim - 1))
    solution = jnp.zeros_like(queries)
    residual = queries
    direction = queries
    norm_now = jnp.sum(residual * residual, axis=-1, keepdims=True)
    for turn_index in range(ITERS):
        operate_from_state = carried * jnp.einsum(
            "...cd,...de->...ce", direction, gram_state, precision=HIGHEST
        )
        operate_correlation = (
            jnp.einsum("...cd,...jd->...cj", direction, normed_keys, precision=HIGHEST) * weights
        )
        mapped = (
            operate_from_state
            + jnp.einsum("...cj,...jd->...cd", operate_correlation, normed_keys, precision=HIGHEST)
            + ridge_term * direction
        )
        step_size = norm_now / jnp.sum(direction * mapped, axis=-1, keepdims=True)
        solution = solution + step_size * direction
        if turn_index + 1 < ITERS:
            residual = residual - step_size * mapped
            norm_next = jnp.sum(residual * residual, axis=-1, keepdims=True)
            direction = residual + norm_next / norm_now * direction
            norm_now = norm_next
    correlation = (
        jnp.einsum("...cd,...jd->...cj", solution, normed_keys, precision=HIGHEST) * weights
    )
    from_state = carried * jnp.einsum("...cd,...de->...ce", solution, memory, precision=HIGHEST)
    return from_state + jnp.einsum("...cj,...je->...ce", correlation, values, precision=HIGHEST)


def local_states(totals, gram_terms, memory_terms):

    def advance(state_pair, inputs):
        gram_state, memory = state_pair
        block_total, gram_term, memory_term = inputs
        factor = jnp.exp(block_total)[:, None, None]
        return (
            (factor * gram_state + gram_term, factor * memory + memory_term),
            (gram_state, memory),
        )

    empty_state = jnp.zeros(gram_terms.shape[:1] + gram_terms.shape[2:], jnp.float32)
    final_pair, starts = lax.scan(
        advance,
        (empty_state, empty_state),
        (totals.T, jnp.moveaxis(gram_terms, 1, 0), jnp.moveaxis(memory_terms, 1, 0)),
    )
    return (
        final_pair[0],
        final_pair[1],
        jnp.moveaxis(starts[0], 0, 1),
        jnp.moveaxis(starts[1], 0, 1),
    )


def combine_states(earlier, later):
    factor = later[0][:, None, None]
    return (earlier[0] * later[0], factor * earlier[1] + later[1], factor * earlier[2] + later[2])


def body(query_rows, key_rows, value_rows, log_decay, regularizer, norm_gain, out_weight):
    heads_here = regularizer.shape[0]
    query_rows, key_rows, value_rows = (
        lax.all_to_all(query_rows, "head", split_axis=1, concat_axis=0, tiled=True),
        lax.all_to_all(key_rows, "head", split_axis=1, concat_axis=0, tiled=True),
        lax.all_to_all(value_rows, "head", split_axis=1, concat_axis=0, tiled=True),
    )
    row_total = key_rows.shape[0]
    normed_keys = unit_keys(to_blocks(key_rows, heads_here))
    values = to_blocks(value_rows, heads_here)
    cumulative = jnp.cumsum(log_decay.reshape(heads_here, row_total // SPAN, SPAN), axis=-1)
    weights = causal_weights(cumulative)
    totals = cumulative[..., -1]
    tail_decay = jnp.exp(totals[..., None] - cumulative)[..., None]
    gram_terms = jnp.einsum(
        "hnca,hncb->hnab", tail_decay * normed_keys, normed_keys, precision=HIGHEST
    )
    memory_terms = jnp.einsum(
        "hnca,hncb->hnab", tail_decay * normed_keys, values, precision=HIGHEST
    )
    gram_end, memory_end, gram_local, memory_local = local_states(totals, gram_terms, memory_terms)
    device_decay = jnp.exp(jnp.sum(totals, axis=-1))
    identity = (jnp.ones_like(device_decay), jnp.zeros_like(gram_end), jnp.zeros_like(memory_end))
    decay_in, gram_in, memory_in = prefix(
        (device_decay, gram_end, memory_end), "seq", combine_states, identity
    )
    before = jnp.exp(jnp.cumsum(totals, axis=-1) - totals)[..., None, None]
    gram_start = before * gram_in[:, None] + gram_local
    memory_start = before * memory_in[:, None] + memory_local
    queries = to_blocks(query_rows, heads_here)
    readout = solve_block(
        queries, normed_keys, values, cumulative, weights, gram_start, memory_start, regularizer
    )
    scale_back = lax.rsqrt(jnp.mean(readout * readout, axis=-1, keepdims=True) + EPSILON)
    normed = (readout * scale_back * norm_gain[:, None, None, :]).astype(jnp.bfloat16)
    readout_rows = jnp.transpose(normed, (1, 2, 0, 3)).reshape(
        row_total, heads_here * normed.shape[-1]
    )
    return lax.psum_scatter(
        jnp.dot(readout_rows, out_weight, preferred_element_type=jnp.float32).astype(jnp.bfloat16),
        "head",
        scatter_dimension=0,
        tiled=True,
    )


def solution(mesh):
    placed = (
        P(("seq", "head"), None),
        P(("seq", "head"), None),
        P(("seq", "head"), None),
        P("head", "seq"),
        P("head"),
        P("head", None),
        P("head", None),
    )
    return jax.shard_map(
        body, mesh=mesh, in_specs=placed, out_specs=P(("seq", "head"), None), check_vma=False
    )
```

profile of v0, /device:TPU:1, one launch (start us, length us, event | category | flops | bytes accessed | tf_op | source)
XLA Modules:
  0.0 571.1 jit_solution(7442901586109338632)
XLA Ops:
  8.4 4.8 all-to-all-start.1
  16.8 3.8 all-to-all-done.1
  20.6 4.1 all-to-all-start.2
  27.3 2.6 copy.184
  32.9 2.7 convolution_bitcast_fusion
  35.6 2.9 convolution_bitcast_fusion.2
  38.4 4.8 while.33
  46.7 3.5 all-to-all-start
  51.5 133.5 %all-reduce = f32[512]{0:T(512)S(1)} all-reduce(f32[512]{0:T(512)S(1)} %exponential_dynamic-update-slice_fusion), channel_id=2, replica_groups=mesh['seq'=64,'head'=4] {'seq'}, use_global_device_ids=true, to_apply=%add | all-reduce | flops 512 | bytes 4096
  192.5 142.3 %all-gather.8.cloned.1.call-done = f32[512,128,128]{2,1,0:T(8,128)} async-done(((f32[8,128,128]{2,1,0:T(8,128)}), f32[512,128,128]{2,1,0:T(8,128)}) %all-gather.8.cloned.1.call-update) | async-done | bytes 33554448 | tf_op jit(solution)/shard_map/all_gather | solution.py:16
  334.8 154.2 %while.34 = (s32[]{:T(128)}, f32[8,128,128]{2,1,0:T(8,128)S(1)}, f32[8,128,128]{2,1,0:T(8,128)}, s32[]{:T(128)}, f32[64,8]{1,0:T(8,128)S(1)}, /*index=5*/f32[64,...) while((s32[]{:T(128)}, f32[8,128,128]{2,1,0:T(8,128)S(1)}, ...), condition=%wide.region_8.9_spmd.clone, body=%wide.region_7.8_spmd.clone.sunk | while | flops 1048580 | bytes 3145945 | solution.py:28
  344.3 2.4 fusion.77
  370.9 2.4 fusion.77
  380.5 2.4 fusion.77
  390.1 2.4 fusion.77
  416.7 2.4 fusion.77
  426.3 2.4 fusion.77
  436.0 2.4 fusion.77
  462.5 2.4 fusion.77
  472.2 2.4 fusion.77
  481.8 2.4 fusion.77
  491.9 2.5 fusion.14
  528.1 7.1 %convolution_convert_fusion = bf16[256,4096]{1,0:T(8,128)(2,1)} fusion(bf16[1024,4096]{1,0:T(8,128)(2,1)} %param.17, bf16[32,8,8,128]{3,2,1,0:T(8,128)(2,1)S(1)} %bitcast.182), kind=kOutput, calls=%fused_computation.13 | convolution fusion | flops 2148532224 | bytes 11010048 | tf_op jit(solution)/shard_map/dot_general | solution.py:156
  535.2 28.9 %reduce-scatter.2.cloned.1.call-done = bf16[64,4096]{1,0:T(8,128)(2,1)} async-done(((bf16[256,4096]{1,0:T(8,128)(2,1)}), bf16[64,4096]{1,0:T(8,128)(2,1)}) %reduce-scatter.2.cloned.1.call-update) | async-done | bytes 524304 | tf_op jit(solution)/shard_map/reduce_scatter | solution.py:155
  (219 shorter events, 193.7 us)
Async XLA Ops:
  8.4 12.2 %all-to-all-start.1 = ((bf16[64,4,1024]{2,0,1:T(8,128)(2,1)}), bf16[64,4,1024]{2,0,1:T(8,128)(2,1)S(1)}, u32[]{:S(2)}, u32[]{:S(2)}) async-start(bf16[64,4,1024]{2,0,1:T(8,128)(2,1)} %bitcast.151), calls=%async_computation.1 | async-start | bytes 1048576 | tf_op jit(solution)/shard_map/all_to_all | solution.py:121
  20.6 11.1 %all-to-all-start.2 = ((bf16[64,4,1024]{2,0,1:T(8,128)(2,1)}), bf16[64,4,1024]{2,0,1:T(8,128)(2,1)}, u32[]{:S(2)}, u32[]{:S(2)}) async-start(bf16[64,4,1024]{2,0,1:T(8,128)(2,1)} %bitcast.150), calls=%async_computation.2 | async-start | bytes 1048576 | tf_op jit(solution)/shard_map/all_to_all | solution.py:122
  24.8 167.8 %all-gather.6.cloned.1.call-start = ((), (), s32[]{:S(2)}) async-start(), calls=%async_computation.5 | async-start | bytes 34078720 | tf_op jit(solution)/shard_map/all_gather | solution.py:16
  32.9 2.7 copy-start.2
  38.4 11.8 %copy-start.7 = (u32[256]{0:T(256)S(1)}, u32[256]{0:T(256)}, u32[]{:S(2)}) copy-start(u32[256]{0:T(256)} %constant.67) | copy-start | bytes 3076
  43.2 0.8 copy-start
  43.2 1.0 copy-start.1
  44.0 290.8 %all-gather.8.cloned.1.call-start = ((), (), s32[]{:S(2)}) async-start(), calls=%async_computation.6 | async-start | bytes 34078720 | tf_op jit(solution)/shard_map/all_gather | solution.py:16
  46.7 138.9 %all-to-all-start = ((bf16[64,4,1024]{2,0,1:T(8,128)(2,1)}), bf16[64,4,1024]{2,0,1:T(8,128)(2,1)S(1)}, u32[]{:S(2)}, u32[]{:S(2)}) async-start(bf16[64,4,1024]{2,0,1:T(8,128)(2,1)} %bitcast.152), calls=%async_computation | async-start | bytes 1048576 | tf_op jit(solution)/shard_map/all_to_all | solution.py:120
  50.1 514.0 %reduce-scatter.2.cloned.1.call-start = ((), (), s32[]{:S(2)}) async-start(), calls=%async_computation.4 | async-start | bytes 2621440 | tf_op jit(solution)/shard_map/reduce_scatter | solution.py:155
  185.6 0.8 copy-start.4
  334.8 157.1 %copy-start.5 = (f32[8]{0:T(128)S(1)}, f32[8]{0:T(128)}, u32[]{:S(2)}) copy-start(f32[8]{0:T(128)} %param.15) | copy-start | bytes 100
  489.0 2.9 copy-start.3
  517.9 9.6 %copy-start.6 = (f32[8,128]{1,0:T(8,128)S(1)}, f32[8,128]{1,0:T(8,128)}, u32[]{:S(2)}) copy-start(f32[8,128]{1,0:T(8,128)} %param.16) | copy-start | bytes 12292
Sparse Core Ops, SparseCore 0:
  44.2 148.3 all-gather.5
  195.3 139.4 all-gather.7
  535.3 28.7 reduce-scatter.1
where the time goes:
time: 578 us; the launch traced here: 571 us
  waiting for transfers between devices  178 us (31%)
  other arithmetic  172 us (30%)
  blocking collectives  133 us (23%)
  matrix products  41.4 us (7%)
  local copies, waits for them, and re-layouts  18.1 us (3%)
  between operations  14.6 us (3%)
  starting transfers between devices  12.6 us (2%)
    select_n x64, other arithmetic, step(): return jax.tree.map(lambda a, b: jnp.where(reached, a, b), new, before)  154 us
    all_gather x2, waiting for transfers between devices, prefix(): everything = jax.tree.map(lambda part: lax.all_gather(part, axis), shard)  143 us
    unnamed x1, blocking collectives  133 us
    reduce_scatter x1, waiting for transfers between devices, body(): lax.psum_scatter(jnp.dot(readout_rows, out_weight, preferred_element_type...  28.9 us
  transfers between devices with their start and end apart: 6, of which 5 were waited for; matrix products, arithmetic and copies ran while one was open for 3% of the time, Pallas kernels for 0%

commit v1 on v0

v1 whole, which is shorter than its diff:
```python
import functools

import jax
import jax.numpy as jnp
from jax import lax
from jax.experimental import pallas as pl
from jax.experimental.pallas import tpu as pltpu
from jax.sharding import PartitionSpec as P

SPAN = 128
ITERS = 4
EPSILON = 1e-06
GROUP = 4
TILE = 512
HIGHEST = lax.Precision.HIGHEST
MESH = pl.DeviceIdType.MESH
F32 = jnp.float32
BF16 = jnp.bfloat16
ROWS_BY_ROWS = (((1,), (1,)), ((), ()))
COLS_BY_COLS = (((0,), (0,)), ((), ()))


def kernel(
    planes, inner, ring,
    q_hbm, k_hbm, v_hbm, ld_ref, reg_ref, gain_ref, w_hbm, out_ref,
    qb, kb, vb, wv, weights, carried, tails, totals, knorm, first,
    dec, dec_plane, dec_ztot, dec_z,
    state_out, state_plane, ptot, z_in, z_out, z_state, back_out, start,
    solved, readout, partial32, partial, relay_a, relay_b, n1_a, n1_b, n2_a, n2_b, comb_a, comb_b,
    local_sem, x_send, x_recv, dp_send, dp_recv, dz_send, dz_recv,
    p_send, p_recv, z_send, z_recv, zb_send, zb_recv, b_send, b_recv, r_send, r_recv,
):
    s = lax.axis_index("seq")
    x = lax.axis_index("head")
    z = lax.div(s, inner)
    me = lax.rem(s, inner)
    rows = q_hbm.shape[0]
    width = kb.shape[1]
    heads = ld_ref.shape[0]
    half = w_hbm.shape[1] // 2
    pending = []

    def to_plane(peer):
        return (z * inner + peer, x)

    def to_z(peer):
        return (peer * inner + me, x)

    def to_x(peer):
        return (s, peer)

    def remote(src, dst, send, recv, device):
        return pltpu.make_async_remote_copy(
            src_ref=src, dst_ref=dst, send_sem=send, recv_sem=recv,
            device_id=device, device_id_type=MESH,
        )

    def exchange(count, here, device, make, send, recv):
        def each(fn):
            def step(o, carry):
                fn(o)
                return carry
            lax.fori_loop(1, count, step, 0)

        def go(o):
            peer = lax.rem(here + o, count)
            src, dst = make(peer, here)
            remote(src, dst, send(o - 1), recv(o - 1), device(peer)).start()

        def got(o):
            peer = lax.rem(here + count - o, count)
            src, dst = make(here, peer)
            remote(src, dst, send(o - 1), recv(o - 1), device(peer)).wait_recv()

        def sent(o):
            peer = lax.rem(here + o, count)
            src, dst = make(peer, here)
            remote(src, dst, send(o - 1), recv(o - 1), device(peer)).wait_send()

        each(go)
        pending.append(lambda: each(sent))
        return lambda: each(got)

    barrier = pltpu.get_barrier_semaphore()
    for count, here, device in ((ring, x, to_x), (inner, me, to_plane), (planes, z, to_z)):
        def greet(o, carry, count=count, here=here, device=device):
            pl.semaphore_signal(
                barrier, inc=1, device_id=device(lax.rem(here + o, count)), device_id_type=MESH
            )
            return carry
        lax.fori_loop(1, count, greet, 0)
    pl.semaphore_wait(barrier, ring + inner + planes - 3)

    x_done = []
    for i, (src_hbm, dst_buf) in enumerate(((k_hbm, kb), (v_hbm, vb), (q_hbm, qb))):
        mine = pltpu.make_async_copy(
            src_hbm.at[:, pl.ds(pl.multiple_of(x * width, width), width)],
            dst_buf.at[pl.ds(pl.multiple_of(x * rows, rows), rows), :],
            local_sem.at[i],
        )
        mine.start()

        def make(to, frm, src_hbm=src_hbm, dst_buf=dst_buf):
            return (
                src_hbm.at[:, pl.ds(pl.multiple_of(to * width, width), width)],
                dst_buf.at[pl.ds(pl.multiple_of(frm * rows, rows), rows), :],
            )

        got = exchange(
            ring, x, to_x, make,
            lambda o, i=i: x_send.at[i, o], lambda o, i=i: x_recv.at[i, o],
        )
        x_done.append((mine, got))
    w_copy = pltpu.make_async_copy(w_hbm, wv, local_sem.at[3])
    w_copy.start()

    row_id = lax.broadcasted_iota(jnp.int32, (SPAN, SPAN), 0)
    col_id = lax.broadcasted_iota(jnp.int32, (SPAN, SPAN), 1)
    causal = row_id >= col_id
    lower = jnp.where(causal, 1.0, 0.0).astype(F32)

    def head_row(table, h):
        place = lax.broadcasted_iota(jnp.int32, table.shape, 0)
        return jnp.sum(jnp.where(place == h, table, 0.0), axis=0, keepdims=True)

    def prepare(h, carry):
        total = None
        for n in range(2):
            spread_row = jnp.broadcast_to(
                head_row(ld_ref[:, n * SPAN:(n + 1) * SPAN], h), (SPAN, SPAN)
            )
            cum = lax.dot_general(
                lower, spread_row, ROWS_BY_ROWS, precision=HIGHEST, preferred_element_type=F32
            )
            cum_row = lax.dot_general(
                spread_row, lower, ROWS_BY_ROWS, precision=HIGHEST, preferred_element_type=F32
            )
            weights[n, h] = jnp.where(causal, jnp.exp(jnp.minimum(cum - cum_row, 0.0)), 0.0)
            carried[n, h] = jnp.exp(cum)
            last = cum[SPAN - 1:SPAN, :]
            tails[n, h] = jnp.exp(last - cum)
            totals[n, h] = jnp.broadcast_to(last, (8, SPAN))
            total = last if total is None else total + last
        dec[h] = jnp.broadcast_to(total, (8, SPAN))
        return carry

    lax.fori_loop(0, heads, prepare, 0)

    got_dec = exchange(
        inner, me, to_plane, lambda to, frm: (dec.at[to], dec_plane.at[frm]),
        lambda o: dp_send.at[o], lambda o: dp_recv.at[o],
    )
    dec_plane[me] = dec[me]
    got_dec()

    dec_ztot[...] = lax.fori_loop(
        0, inner, lambda i, acc: acc + dec_plane[i], jnp.zeros((8, SPAN), F32)
    )
    got_decz = exchange(
        planes, z, to_z, lambda to, frm: (dec_ztot, dec_z.at[frm]),
        lambda o: dz_send.at[o], lambda o: dz_recv.at[o],
    )
    dec_z[z] = dec_ztot[...]
    got_decz()

    def wait_x(i):
        mine, got = x_done[i]
        mine.wait()
        got()

    def head_cols(h):
        return pl.ds(pl.multiple_of(h * SPAN, SPAN), SPAN)

    def local_state(t):
        def one(h, carry):
            terms = []
            for n in range(2):
                if t == 0:
                    key = kb[n * SPAN:(n + 1) * SPAN, head_cols(h)].astype(F32)
                    square = jnp.mean(key * key, axis=-1, keepdims=True)
                    normed = key * (lax.rsqrt(square + EPSILON) * SPAN ** -0.5)
                    right = normed.astype(BF16)
                    knorm[n, h] = right
                    tails[n, h] = tails[n, h] * normed
                else:
                    right = vb[n * SPAN:(n + 1) * SPAN, head_cols(h)]
                terms.append(
                    lax.dot_general(
                        tails[n, h].astype(BF16), right, COLS_BY_COLS, preferred_element_type=F32
                    )
                )
            first[t, h] = terms[0]
            factor = jnp.exp(totals[1, h][0:1, :])
            state_out[t, h] = (factor * terms[0] + terms[1]).astype(BF16)
            return carry

        lax.fori_loop(0, heads, one, 0)

    def send_plane(t):
        got = exchange(
            inner, me, to_plane,
            lambda to, frm: (state_out.at[t, to], state_plane.at[t, frm]),
            lambda o: p_send.at[t, o], lambda o: p_recv.at[t, o],
        )
        state_plane[t, me] = state_out[t, me]
        return got

    def plane_total(t):
        def step(i, acc):
            return jnp.exp(dec_plane[i][0:1, :]) * acc + state_plane[t, i].astype(F32)

        ptot[t] = lax.fori_loop(0, inner, step, jnp.zeros((SPAN, SPAN), F32)).astype(BF16)

    piece = SPAN // planes

    def piece_rows(i):
        return pl.ds(pl.multiple_of(i * piece, piece), piece)

    def send_z(t):
        got = exchange(
            planes, z, to_z,
            lambda to, frm: (ptot.at[t, piece_rows(to), :], z_in.at[t, frm]),
            lambda o: z_send.at[t, o], lambda o: z_recv.at[t, o],
        )
        z_in[t, z] = ptot[t, piece_rows(z), :]
        return got

    def z_prefix(t):
        def step(i, acc):
            z_out[t, i] = acc.astype(BF16)
            return jnp.exp(dec_z[i][0:1, :]) * acc + z_in[t, i].astype(F32)

        lax.fori_loop(0, planes, step, jnp.zeros((piece, SPAN), F32))

    def send_z_back(t):
        got = exchange(
            planes, z, to_z,
            lambda to, frm: (z_out.at[t, to], z_state.at[t, piece_rows(frm), :]),
            lambda o: zb_send.at[t, o], lambda o: zb_recv.at[t, o],
        )
        z_state[t, piece_rows(z), :] = z_out[t, z]
        return got

    def plane_prefix(t):
        def step(i, acc):
            back_out[t, i] = acc.astype(BF16)
            return jnp.exp(dec_plane[i][0:1, :]) * acc + state_plane[t, i].astype(F32)

        lax.fori_loop(0, inner, step, z_state[t].astype(F32))

    def send_back(t):
        got = exchange(
            inner, me, to_plane,
            lambda to, frm: (back_out.at[t, to], start.at[t, frm]),
            lambda o: b_send.at[t, o], lambda o: b_recv.at[t, o],
        )
        start[t, me] = back_out[t, me]
        return got

    wait_x(0)
    local_state(0)
    got_p0 = send_plane(0)
    got_p0()
    plane_total(0)
    got_z0 = send_z(0)
    wait_x(1)
    local_state(1)
    got_p1 = send_plane(1)
    got_z0()
    z_prefix(0)
    got_zb0 = send_z_back(0)
    got_p1()
    plane_total(1)
    got_z1 = send_z(1)
    got_zb0()
    plane_prefix(0)
    got_b0 = send_back(0)
    got_z1()
    z_prefix(1)
    got_zb1 = send_z_back(1)
    got_zb1()
    plane_prefix(1)
    got_b1 = send_back(1)
    got_b0()
    wait_x(2)
    def block_rows(n):
        return pl.ds(pl.multiple_of(n * SPAN, SPAN), SPAN)

    def start_state(t, n, h):
        later = jnp.where(n == 1, 1.0, 0.0).astype(F32)
        factor = jnp.where(n == 1, jnp.exp(totals[0, h][0:1, :]), 1.0)
        return (factor * start[t, h].astype(F32) + later * first[t, h]).astype(BF16)

    def row_sum(a):
        return jnp.sum(a, axis=-1, keepdims=True)

    def solve(n):
        def solve_group(g, carry):
            hs = [g * GROUP + i for i in range(GROUP)]
            each = range(GROUP)
            keys = [knorm[n, h] for h in hs]
            mixed = [jnp.concatenate([start_state(0, n, h), knorm[n, h]], axis=0) for h in hs]
            direction = [qb[block_rows(n), head_cols(h)].astype(F32) for h in hs]
            residual = list(direction)
            answer = [None] * GROUP
            norm_now = [row_sum(r * r) for r in residual]
            for turn in range(ITERS):
                corr = [
                    lax.dot_general(
                        direction[i].astype(BF16), keys[i], ROWS_BY_ROWS,
                        preferred_element_type=F32,
                    )
                    for i in each
                ]
                left = [
                    jnp.concatenate(
                        [
                            (carried[n, hs[i]] * direction[i]).astype(BF16),
                            (corr[i] * weights[n, hs[i]]).astype(BF16),
                        ],
                        axis=1,
                    )
                    for i in each
                ]
                mapped = [
                    jnp.dot(left[i], mixed[i], preferred_element_type=F32)
                    + reg_ref[hs[i]] * direction[i]
                    for i in each
                ]
                step_size = [norm_now[i] / row_sum(direction[i] * mapped[i]) for i in each]
                answer = [
                    step_size[i] * direction[i]
                    if turn == 0
                    else answer[i] + step_size[i] * direction[i]
                    for i in each
                ]
                if turn + 1 < ITERS:
                    residual = [residual[i] - step_size[i] * mapped[i] for i in each]
                    norm_next = [row_sum(r * r) for r in residual]
                    direction = [
                        residual[i] + norm_next[i] / norm_now[i] * direction[i] for i in each
                    ]
                    norm_now = norm_next
            for i in each:
                solved[g * GROUP + i] = answer[i]
            return carry

        lax.fori_loop(0, heads // GROUP, solve_group, 0)

    def read(n):
        def read_group(g, carry):
            hs = [g * GROUP + i for i in range(GROUP)]
            for h in hs:
                answer = solved[h]
                corr = lax.dot_general(
                    answer.astype(BF16), knorm[n, h], ROWS_BY_ROWS, preferred_element_type=F32
                )
                left = jnp.concatenate(
                    [
                        (carried[n, h] * answer).astype(BF16),
                        (corr * weights[n, h]).astype(BF16),
                    ],
                    axis=1,
                )
                mixed = jnp.concatenate(
                    [start_state(1, n, h), vb[block_rows(n), head_cols(h)]], axis=0
                )
                raw = jnp.dot(left, mixed, preferred_element_type=F32)
                scale = lax.rsqrt(jnp.mean(raw * raw, axis=-1, keepdims=True) + EPSILON)
                readout[:, head_cols(h)] = (raw * scale * head_row(gain_ref[...], h)).astype(BF16)
            return carry

        lax.fori_loop(0, heads // GROUP, read_group, 0)

    def project(lo, hi):
        def tile(c, carry):
            cols = pl.ds(pl.multiple_of(c * TILE, TILE), TILE)
            partial32[:, cols] = jnp.dot(
                readout[...], wv[:, cols], preferred_element_type=F32
            )
            return carry

        lax.fori_loop(lo // TILE, hi // TILE, tile, 0)

    far, near_1, near_2 = x ^ 2, x ^ 3, x ^ 1
    r_done = {}

    def slot(chunk):
        return pl.ds(pl.multiple_of(lax.rem(chunk, 2) * rows, rows), rows)

    def columns(side):
        return slice(0, half) if side == 0 else slice(half, 2 * half)

    def send_result(i, src, dst, peer):
        copy = remote(src, dst, r_send.at[i], r_recv.at[i], to_x(peer))
        copy.start()
        pending.append(copy.wait_send)
        r_done[i] = copy.wait_recv

    n = 1 - lax.div(x, 2)
    solve(n)
    got_b1()
    read(n)
    w_copy.wait()
    for side in range(2):
        project(side * half, (side + 1) * half)
        partial[0, :, columns(side)] = partial32[:, columns(side)].astype(BF16)
        src = partial.at[0, slot(far), columns(side)]
        if side == 0:
            send_result(0, src, relay_a, near_1)
            send_result(1, partial.at[0, slot(near_1), columns(0)], n1_a, near_1)
        else:
            send_result(2, src, relay_b, near_2)

    n = lax.div(x, 2)
    solve(n)
    read(n)
    r_done.pop(2)()
    comb_b[...] = (
        partial[0, slot(near_1), columns(1)].astype(F32) + relay_b[...].astype(F32)
    ).astype(BF16)
    send_result(3, comb_b, n1_b, near_1)
    project(half, 2 * half)
    partial[1, :, columns(1)] = partial32[:, columns(1)].astype(BF16)
    send_result(4, partial.at[1, slot(near_2), columns(1)], n2_b, near_2)
    project(0, half)
    r_done.pop(0)()
    comb_a[...] = (partial32[slot(near_2), columns(0)] + relay_a[...].astype(F32)).astype(BF16)
    send_result(5, comb_a, n2_a, near_2)
    for i in (1, 3, 4, 5):
        r_done.pop(i)()
    out_ref[:, columns(0)] = (
        partial32[slot(x), columns(0)] + n1_a[...].astype(F32) + n2_a[...].astype(F32)
    ).astype(BF16)
    out_ref[:, columns(1)] = (
        partial32[slot(x), columns(1)] + n1_b[...].astype(F32) + n2_b[...].astype(F32)
    ).astype(BF16)
    for fn in pending:
        fn()


def body(planes, inner, query_rows, key_rows, value_rows, log_decay, regularizer, norm_gain, out_weight):
    ring = lax.axis_size("head")
    rows, model = query_rows.shape
    heads = regularizer.shape[0]
    width = heads * SPAN
    tokens = rows * ring
    half = model // 2
    vm = pltpu.VMEM
    dma = pltpu.SemaphoreType.DMA
    piece = SPAN // planes
    scratch = [
        vm((tokens, width), BF16),
        vm((tokens, width), BF16),
        vm((tokens, width), BF16),
        vm((width, model), BF16),
        vm((2, heads, SPAN, SPAN), F32),
        vm((2, heads, SPAN, SPAN), F32),
        vm((2, heads, SPAN, SPAN), F32),
        vm((2, heads, 8, SPAN), F32),
        vm((2, heads, SPAN, SPAN), BF16),
        vm((2, heads, SPAN, SPAN), F32),
        vm((heads, 8, SPAN), F32),
        vm((inner, 8, SPAN), F32),
        vm((8, SPAN), F32),
        vm((planes, 8, SPAN), F32),
        vm((2, heads, SPAN, SPAN), BF16),
        vm((2, inner, SPAN, SPAN), BF16),
        vm((2, SPAN, SPAN), BF16),
        vm((2, planes, piece, SPAN), BF16),
        vm((2, planes, piece, SPAN), BF16),
        vm((2, SPAN, SPAN), BF16),
        vm((2, inner, SPAN, SPAN), BF16),
        vm((2, heads, SPAN, SPAN), BF16),
        vm((heads, SPAN, SPAN), F32),
        vm((SPAN, width), BF16),
        vm((SPAN, model), F32),
        vm((2, SPAN, model), BF16),
    ]
    scratch += [vm((rows, half), BF16)] * 8
    scratch += [dma((4,)), dma((3, ring - 1)), dma((3, ring - 1))]
    scratch += [dma((inner - 1,))] * 2 + [dma((planes - 1,))] * 2
    scratch += [dma((2, inner - 1))] * 2 + [dma((2, planes - 1))] * 4 + [dma((2, inner - 1))] * 2
    scratch += [dma((6,))] * 2
    anywhere = pl.BlockSpec(memory_space=pl.ANY)
    local = pl.BlockSpec(memory_space=pltpu.VMEM)
    return pl.pallas_call(
        functools.partial(kernel, planes, inner, ring),
        out_shape=jax.ShapeDtypeStruct((rows, model), BF16),
        in_specs=[
            anywhere, anywhere, anywhere, local,
            pl.BlockSpec(memory_space=pltpu.SMEM), local, anywhere,
        ],
        out_specs=local,
        scratch_shapes=scratch,
        compiler_params=pltpu.CompilerParams(
            collective_id=0, has_side_effects=True, vmem_limit_bytes=48 * 1024 * 1024
        ),
    )(query_rows, key_rows, value_rows, log_decay, regularizer, norm_gain, out_weight)


def solution(mesh):
    placed = (
        P(("seq", "head"), None),
        P(("seq", "head"), None),
        P(("seq", "head"), None),
        P("head", "seq"),
        P("head"),
        P("head", None),
        P("head", None),
    )
    inner = 8
    planes = mesh.shape["seq"] // inner
    return jax.shard_map(
        functools.partial(body, planes, inner), mesh=mesh, in_specs=placed,
        out_specs=P(("seq", "head"), None), check_vma=False,
    )
```

time: 578 us -> 85.1 us (0.15); the launches traced: 571 us -> 84.8 us
  waiting for transfers between devices: 178 us -> 0 us
  other arithmetic: 172 us -> 0 us
  blocking collectives: 133 us -> 0 us
  Pallas kernels: 0 us -> 78.8 us
  matrix products: 41.4 us -> 0 us
  between operations: 14.6 us -> 0.02 us
  starting transfers between devices: 12.6 us -> 0 us
  local copies, waits for them, and re-layouts: 18.1 us -> 5.96 us
    select_n x64 -> x0, other arithmetic: 154 us -> none  [step(): return jax.tree.map(lambda a, b: jnp.where(reached, a, b), new, before)]
    all_gather x2 -> x0, waiting for transfers between devices: 143 us -> none  [prefix(): everything = jax.tree.map(lambda part: lax.all_gather(part, axis), shard)]
    unnamed x1 -> x0, blocking collectives: 133 us -> none
    pallas_call x0 -> x1, Pallas kernels: none -> 78.8 us  [body(): pl.pallas_call(functools.partial(kernel, planes, inner, ring), out_shape=...]
    dot_general x18 -> x0, matrix products: 41.4 us -> none  [the longest x4 9.19 us: solve_block(): jnp.einsum('...cd,...jd->...cj', direction, normed_keys, precision=HIGHEST)]
    reduce_scatter x1 -> x0, waiting for transfers between devices: 28.9 us -> none  [body(): lax.psum_scatter(jnp.dot(readout_rows, out_weight, preferred_element_type...]
    all_to_all x3 -> x0, starting transfers between devices: 12.4 us -> none  [the longest x1 4.84 us: body(): lax.all_to_all(key_rows, 'head', split_axis=1, concat_axis=0, tiled=True)]
    add x7 -> x0, other arithmetic: 7.98 us -> none  [the longest x2 2.58 us: advance(): factor * memory + memory_term]
  transfers between devices with their start and end apart: 6 -> 0, of which waited for: 5 -> 0; matrix products, arithmetic and copies ran while one was open for 3% -> 0% of each run, Pallas kernels for 0% -> 0%
where the time goes in v1:
time: 85.1 us; the launch traced here: 84.8 us
  Pallas kernels  78.8 us (93%)
  local copies, waits for them, and re-layouts  5.96 us (7%)
    pallas_call x1, Pallas kernels, body(): pl.pallas_call(functools.partial(kernel, planes, inner, ring), out_shape=...  78.8 us
    unnamed x13, local copies, waits for them, and re-layouts  5.96 us

profile of v1, /device:TPU:1, one launch (start us, length us, event | category | flops | bytes accessed | tf_op | source)
XLA Modules:
  0.0 84.8 jit_solution(3278114985557919003)
XLA Ops:
  0.0 0.0 copy-start
  0.0 1.0 %copy-done = bf16[64,4096]{1,0:T(8,128)(2,1)S(1)} copy-done((bf16[64,4096]{1,0:T(8,128)(2,1)S(1)}, bf16[64,4096]{1,0:T(8,128)(2,1)}, u32[]{:S(2)}) %copy-start) | copy-done | bytes 524312
  1.0 0.0 copy-start.1
  1.0 1.0 %copy-done.1 = bf16[64,4096]{1,0:T(8,128)(2,1)S(1)} copy-done((bf16[64,4096]{1,0:T(8,128)(2,1)S(1)}, bf16[64,4096]{1,0:T(8,128)(2,1)}, u32[]{:S(2)}) %copy-start.1) | copy-done | bytes 524312
  2.1 0.0 copy-start.2
  2.1 1.0 %copy-done.2 = bf16[64,4096]{1,0:T(8,128)(2,1)S(1)} copy-done((bf16[64,4096]{1,0:T(8,128)(2,1)S(1)}, bf16[64,4096]{1,0:T(8,128)(2,1)}, u32[]{:S(2)}) %copy-start.2) | copy-done | bytes 524312
  3.1 0.0 copy-start.3
  3.1 0.7 copy-done.3
  3.8 0.0 copy-start.4
  3.8 0.7 copy-done.4
  4.5 0.0 copy-start.5
  4.5 0.7 copy-done.5
  5.2 78.8 %shard_map.73 = bf16[64,4096]{1,0:T(8,128)(2,1)S(1)} custom-call(bf16[64,4096]{1,0:T(8,128)(2,1)S(1)} %copy-done, bf16[64,4096]{1,0:T(8,128)(2,1)S(1)} %copy-done.1, bf16[64,4096]{1,0:T(8,128)(2,1)S(1)} %copy-done.2, f32[8,256]{1,0:T(8,128)S(1)} %copy-done.3, f32[8]{0:T(128)S(1)} %copy-done.5, f32[8,128]{1,0:T(8,128)S(1)} %copy-done.4, bf16[1024,4096]{1,0:T(8,128)(2,1)} %w_hbm.1), custom_call_target="tpu_custom_call" | custom-call | tf_op jit(solution)/shard_map/pallas_call | solution.py:487
  84.0 0.8 copy.9
Async XLA Ops:
  0.0 1.0 %copy-start = (bf16[64,4096]{1,0:T(8,128)(2,1)S(1)}, bf16[64,4096]{1,0:T(8,128)(2,1)}, u32[]{:S(2)}) copy-start(bf16[64,4096]{1,0:T(8,128)(2,1)} %q_hbm.1) | copy-start | bytes 1572868
  1.0 1.0 %copy-start.1 = (bf16[64,4096]{1,0:T(8,128)(2,1)S(1)}, bf16[64,4096]{1,0:T(8,128)(2,1)}, u32[]{:S(2)}) copy-start(bf16[64,4096]{1,0:T(8,128)(2,1)} %k_hbm.1) | copy-start | bytes 1572868
  2.1 1.0 %copy-start.2 = (bf16[64,4096]{1,0:T(8,128)(2,1)S(1)}, bf16[64,4096]{1,0:T(8,128)(2,1)}, u32[]{:S(2)}) copy-start(bf16[64,4096]{1,0:T(8,128)(2,1)} %v_hbm.1) | copy-start | bytes 1572868
  3.1 0.7 copy-start.3
  3.8 0.7 copy-start.4
  4.5 0.7 copy-start.5

commit v2 on v0

v2 whole, which is shorter than its diff:
```python
import functools

import jax
import jax.numpy as jnp
from jax import lax
from jax.experimental import pallas as pl
from jax.experimental.pallas import tpu as pltpu
from jax.sharding import PartitionSpec as P

SPAN = 128
ITERS = 4
EPSILON = 1e-06
TILE = 512
BATCH = 2
MESH = pl.DeviceIdType.MESH
HIGHEST = lax.Precision.HIGHEST
F32 = jnp.float32
BF16 = jnp.bfloat16
ROWS_BY_ROWS = (((1,), (1,)), ((), ()))
COLS_BY_COLS = (((0,), (0,)), ((), ()))


def kernel(
    planes, inner, ring,
    q_hbm, k_hbm, v_hbm, ld_hbm, reg_hbm, gain_hbm, w_hbm, out_ref,
    ld_plane, reg_ref, gain_ref, qb, kb, vb, wv, weights, carried, tails, leave, enter, dec_total,
    knorm, klow, tailed, terms, before, z_to, z_in, z_out, z_back, z_state,
    solved, sending, readout, own, partial,
    relay_a, relay_b, n1_a, n1_b, n2_a, n2_b,
    local_sem, ld_send, ld_recv, g_send, g_recv,
    z_send, z_recv, zb_send, zb_recv, b_send, b_recv, r_send, r_recv,
):
    s = lax.axis_index("seq")
    x = lax.axis_index("head")
    z = lax.div(s, inner)
    me = lax.rem(s, inner)
    rows = q_hbm.shape[0]
    blocks = knorm.shape[0]
    per_device = blocks // inner
    half = w_hbm.shape[1] // 2
    pending = []

    def loop(lo, hi, fn):
        def step(i, carry):
            fn(i)
            return carry
        lax.fori_loop(lo, hi, step, 0)

    def shift_plane(o, sign):
        return lax.rem(me + inner + sign * o, inner)

    def shift_z(o, sign):
        return lax.rem(z + planes + sign * o, planes)

    def shift_group(o, sign):
        over = lax.div(o, ring)
        along = lax.rem(o, ring)
        return (
            lax.rem(me + inner + sign * over, inner), lax.rem(x + ring + sign * along, ring)
        )

    def shift_far(mask):
        return lambda o, sign: (lax.rem(me + inner + sign * o, inner), x ^ mask)

    def in_group(peer):
        return (z * inner + peer[0], peer[1])

    plane = (1, inner, shift_plane, lambda peer: (z * inner + peer, x))
    column = (1, planes, shift_z, lambda peer: (peer * inner + me, x))
    group = (1, inner * ring, shift_group, in_group)
    kinds = [(0 if mask else 1, inner, shift_far(mask), in_group) for mask in (2, 3, 1, 0)]

    def remote(src, dst, send, recv, device):
        return pltpu.make_async_remote_copy(
            src_ref=src, dst_ref=dst, send_sem=send, recv_sem=recv,
            device_id=device, device_id_type=MESH,
        )

    def exchange(partners, make_pair, send, recv, here, later=False):
        first, count, shift, device = partners

        def copy(o, sign):
            peer = shift(o, sign)
            src, dst = make_pair(peer, here) if sign == 1 else make_pair(here, peer)
            return remote(src, dst, send(o), recv(o), device(peer))

        pending.append(lambda: loop(first, count, lambda o: copy(o, 1).wait_send()))
        if later:
            return (lambda o: copy(o, 1).start()), (lambda o: copy(o, -1).wait_recv())
        loop(first, count, lambda o: copy(o, 1).start())
        return lambda o: copy(o, -1).wait_recv()

    def all_of(partners, got):
        loop(partners[0], partners[1], got)

    small = [
        pltpu.make_async_copy(src, dst, local_sem.at[i])
        for i, (src, dst) in enumerate(
            ((ld_hbm, ld_plane.at[me]), (reg_hbm, reg_ref), (gain_hbm, gain_ref))
        )
    ]
    for copy in small:
        copy.start()

    barrier = pltpu.get_barrier_semaphore()
    for _, count, shift, device in (group, column):
        loop(
            1, count,
            lambda o, shift=shift, device=device: pl.semaphore_signal(
                barrier, inc=1, device_id=device(shift(o, 1)), device_id_type=MESH
            ),
        )
    pl.semaphore_wait(barrier, inner * ring - 1 + planes - 1)

    got_ld = exchange(
        plane, lambda to, frm: (ld_hbm, ld_plane.at[frm]),
        lambda o: ld_send.at[o], lambda o: ld_recv.at[o], me,
    )

    def slot(place):
        return pl.ds(pl.multiple_of((place[0] * ring + place[1]) * rows, rows), rows)

    def head_cols(place):
        return pl.ds(pl.multiple_of((place[1] * inner + place[0]) * SPAN, SPAN), SPAN)

    got_group = []
    for i, (src_hbm, dst_buf) in enumerate(((k_hbm, kb), (v_hbm, vb), (q_hbm, qb))):
        def make(to, frm, src_hbm=src_hbm, dst_buf=dst_buf):
            return src_hbm.at[:, head_cols(to)], dst_buf.at[slot(frm), :]

        mine = pltpu.make_async_copy(*make((me, x), (me, x)), local_sem.at[3 + i])
        mine.start()
        parts = [group] if i < 2 else kinds
        moves = [
            exchange(
                part, make,
                lambda o, i=i, at=n * inner: g_send.at[i, at + o],
                lambda o, i=i, at=n * inner: g_recv.at[i, at + o],
                (me, x), later=True,
            )
            for n, part in enumerate(parts)
        ]
        got_group.append((mine, moves))

    def go_group(i, n=0):
        part = group if i < 2 else kinds[n]
        loop(part[0], part[1], got_group[i][1][n][0])

    go_group(0)
    go_group(1)
    w_copy = pltpu.make_async_copy(w_hbm, wv, local_sem.at[6])

    def pick_row(table, i):
        place = lax.broadcasted_iota(jnp.int32, table.shape, 0)
        return jnp.sum(jnp.where(place == i, table, 0.0), axis=0, keepdims=True)

    row_id = lax.broadcasted_iota(jnp.int32, (SPAN, SPAN), 0)
    col_id = lax.broadcasted_iota(jnp.int32, (SPAN, SPAN), 1)
    causal = row_id >= col_id
    for copy in small:
        copy.wait()
    all_of(plane, got_ld)

    def down(row):
        return jnp.transpose(jnp.broadcast_to(row, (SPAN, SPAN)))

    sums = lax.dot_general(
        jnp.concatenate(
            [
                pick_row(ld_plane[b // per_device][:, (b % per_device) * SPAN:(b % per_device + 1) * SPAN], me)
                for b in range(blocks)
            ],
            axis=0,
        ),
        jnp.where(causal, 1.0, 0.0).astype(F32),
        ROWS_BY_ROWS, precision=HIGHEST, preferred_element_type=F32,
    )
    total = jnp.zeros((8, SPAN), F32)
    for b in range(blocks):
        row = sums[b:b + 1, :]
        last = jnp.broadcast_to(row[:, SPAN - 1:SPAN], (8, SPAN))
        enter[b] = jnp.exp(total)
        total = total + last
        cum = down(row)
        tails[b] = jnp.exp(last[0:1, :] - cum)
        weights[b] = jnp.where(causal, jnp.exp(jnp.minimum(cum - row, 0.0)), 0.0)
        carried[b] = jnp.exp(cum)
        leave[b] = jnp.exp(last)
    dec_total[...] = total

    def split(value):
        high = value.astype(BF16)
        return high, (value - high.astype(F32)).astype(BF16)

    def block_rows(b):
        return pl.ds(pl.multiple_of(b * SPAN, SPAN), SPAN)

    def plane_states(t):
        mine, ((_, got),) = got_group[t]

        def states(over):
            source = lax.rem(me + inner - over, inner)
            for n in range(per_device):
                b = source * per_device + n
                if t == 0:
                    key = kb[block_rows(b), :].astype(F32)
                    square = jnp.mean(key * key, axis=-1, keepdims=True)
                    normed = key * (lax.rsqrt(square + EPSILON) * SPAN ** -0.5)
                    right, right_low = split(normed)
                    knorm[b] = right
                    klow[b] = right_low
                    left, left_low = split(tails[b] * normed)
                    tailed[b] = left
                    left = jnp.concatenate([left, left_low, left], axis=0)
                    right = jnp.concatenate([right, right, right_low], axis=0)
                else:
                    right = vb[block_rows(b), :]
                    left = tailed[b]
                terms[b] = lax.dot_general(
                    left, right, COLS_BY_COLS, preferred_element_type=F32
                )

        def batch(i):
            if isinstance(i, int):
                mine.wait()
                loop(1, BATCH * ring, got)
            else:
                loop(i * BATCH * ring, (i + 1) * BATCH * ring, got)
            for n in range(BATCH):
                states(i * BATCH + n)

        batch(0)
        loop(1, inner // BATCH, batch)
        plane_total = jnp.zeros((SPAN, SPAN), F32)
        for b in range(blocks):
            before[t, b] = plane_total
            plane_total = leave[b][0:1, :] * plane_total + terms[b]
        for i in range(planes):
            rows_of = plane_total[i * piece:(i + 1) * piece, :]
            if t == 0:
                z_to[i, 0:piece, :], z_to[i, piece:2 * piece, :] = split(rows_of)
            else:
                z_to[i, 2 * piece:3 * piece, :] = rows_of.astype(BF16)

    piece = SPAN // planes

    def send_z():
        rest = dec_total[0:1, :]
        terms_of = []
        for _ in range(3):
            term = rest.astype(BF16)
            terms_of.append(jnp.broadcast_to(term.astype(F32), (8, SPAN)))
            rest = rest - term.astype(F32)
        place = lax.broadcasted_iota(jnp.int32, (piece, SPAN), 0)
        packed = jnp.zeros((piece, SPAN), F32)
        for i, term in enumerate(terms_of):
            packed = jnp.where(place == i, term[0:1, :], packed)
        packed = packed.astype(BF16)
        for i in range(planes):
            z_to[i, 3 * piece:4 * piece, :] = packed
        got = exchange(
            column, lambda to, frm: (z_to.at[to], z_in.at[frm]),
            lambda o: z_send.at[o], lambda o: z_recv.at[o], z,
        )
        z_in[z] = z_to[z]
        return got

    def z_prefix():
        gram = jnp.zeros((piece, SPAN), F32)
        memory = gram
        for i in range(planes):
            z_out[i, 0:piece, :], z_out[i, piece:2 * piece, :] = split(gram)
            z_out[i, 2 * piece:3 * piece, :] = memory.astype(BF16)
            if i + 1 < planes:
                arrived = z_in[i].astype(F32)
                tail = arrived[3 * piece:4 * piece, :]
                decay = jnp.exp(tail[0:1, :] + tail[1:2, :] + tail[2:3, :])
                gram = decay * gram + (arrived[0:piece, :] + arrived[piece:2 * piece, :])
                memory = decay * memory + arrived[2 * piece:3 * piece, :]

    def send_z_back():
        got = exchange(
            column, lambda to, frm: (z_out.at[to], z_back.at[frm]),
            lambda o: zb_send.at[o], lambda o: zb_recv.at[o], z,
        )
        z_back[z] = z_out[z]
        return got

    def collect():
        for i in range(planes):
            arrived = z_back[i].astype(F32)
            here = slice(i * piece, (i + 1) * piece)
            z_state[0, here, :] = arrived[0:piece, :] + arrived[piece:2 * piece, :]
            z_state[1, here, :] = arrived[2 * piece:3 * piece, :]

    def wait_queries(kind):
        mine, moves = got_group[2]
        if kind == 3:
            mine.wait()
        all_of(kinds[kind], moves[kind][1])

    plane_states(0)
    plane_states(1)
    got_z = send_z()
    for kind in range(4):
        go_group(2, kind)
    all_of(column, got_z)
    z_prefix()
    got_zb = send_z_back()
    w_copy.start()
    wait_queries(0)
    all_of(column, got_zb)
    collect()

    def start_state(t, b):
        return enter[b][0:1, :] * z_state[t] + before[t, b]

    def row_sum(a):
        return jnp.sum(a, axis=-1, keepdims=True)

    chunks = [x ^ mask for mask in (2, 3, 1, 0)]

    def member(i):
        return lax.rem(me + 1 + i, inner)

    def block_of(kind, i):
        return member(i) * per_device + lax.div(chunks[kind], ring // per_device)

    def token_rows(kind):
        return pl.ds(
            pl.multiple_of(lax.rem(chunks[kind], ring // per_device) * rows, rows), rows
        )

    def correlate(vector, b):
        high, low = split(vector)
        key = knorm[b]
        return lax.dot_general(
            jnp.concatenate([high, low], axis=1), jnp.concatenate([key, key], axis=1),
            ROWS_BY_ROWS, preferred_element_type=F32,
        ) + lax.dot_general(high, klow[b], ROWS_BY_ROWS, preferred_element_type=F32)

    def solve(kind):
        each = range(inner)
        bs = [block_of(kind, i) for i in each]
        here = token_rows(kind)
        ridge = reg_ref[me]
        states = [split(start_state(0, b)) for b in bs]
        mixed = [
            jnp.concatenate([states[i][0], knorm[bs[i]], states[i][0], knorm[bs[i]]], axis=0)
            for i in each
        ]
        mixed_low = [jnp.concatenate([states[i][1], klow[bs[i]]], axis=0) for i in each]
        direction = [qb[slot((member(i), chunks[kind])), :].astype(F32) for i in each]
        residual = list(direction)
        answer = [None] * inner
        norm_now = [row_sum(r * r) for r in residual]
        for turn in range(ITERS):
            corr = [correlate(direction[i], bs[i]) for i in each]
            from_state = [split(carried[bs[i], here, :] * direction[i]) for i in each]
            from_block = [split(corr[i] * weights[bs[i], here, :]) for i in each]
            high = [
                jnp.concatenate([from_state[i][0], from_block[i][0]], axis=1) for i in each
            ]
            both = [
                jnp.concatenate([high[i], from_state[i][1], from_block[i][1]], axis=1)
                for i in each
            ]
            mapped = [
                jnp.dot(both[i], mixed[i], preferred_element_type=F32)
                + jnp.dot(high[i], mixed_low[i], preferred_element_type=F32)
                + ridge * direction[i]
                for i in each
            ]
            step_size = [norm_now[i] / row_sum(direction[i] * mapped[i]) for i in each]
            answer = [
                step_size[i] * direction[i]
                if turn == 0
                else answer[i] + step_size[i] * direction[i]
                for i in each
            ]
            if turn + 1 < ITERS:
                residual = [residual[i] - step_size[i] * mapped[i] for i in each]
                norm_next = [row_sum(r * r) for r in residual]
                direction = [
                    residual[i] + norm_next[i] / norm_now[i] * direction[i] for i in each
                ]
                norm_now = norm_next
        for i in each:
            solved[kind, i] = answer[i]

    b_done = {}

    def state_cols(place):
        return pl.ds(pl.multiple_of(place * SPAN, SPAN), SPAN)

    def read(kind):
        gain = pick_row(gain_ref[...], me)
        here = token_rows(kind)
        for i in range(inner):
            o = i + 1
            b = block_of(kind, i)
            answer = solved[kind, i]
            corr = correlate(answer, b)
            left = jnp.concatenate(
                [
                    (carried[b, here, :] * answer).astype(BF16),
                    (corr * weights[b, here, :]).astype(BF16),
                ],
                axis=1,
            )
            mixed = jnp.concatenate([start_state(1, b).astype(BF16), vb[block_rows(b), :]], axis=0)
            raw = jnp.dot(left, mixed, preferred_element_type=F32)
            scale = lax.rsqrt(jnp.mean(raw * raw, axis=-1, keepdims=True) + EPSILON)
            normed = (raw * scale * gain).astype(BF16)
            if o == inner:
                readout[kind, :, state_cols(me)] = normed
            else:
                sending[kind, i] = normed
                copy = remote(
                    sending.at[kind, i], readout.at[kind, :, state_cols(me)],
                    b_send.at[kind, o], b_recv.at[kind, o], plane[3](shift_plane(o, 1)),
                )
                copy.start()
                pending.append(copy.wait_send)
                back = shift_plane(o, -1)
                b_done[kind, o] = remote(
                    sending.at[kind, i], readout.at[kind, :, state_cols(back)],
                    b_send.at[kind, o], b_recv.at[kind, o], plane[3](back),
                ).wait_recv

    def wait_readout(kind):
        for o in range(1, inner):
            b_done.pop((kind, o))()

    tiles = half // TILE
    far, near_1, near_2, _ = chunks

    def tile_cols(side, c):
        return slice(side * half + c * TILE, side * half + (c + 1) * TILE)

    def project(kind, side, c):
        return jnp.dot(
            readout[kind], wv[:, tile_cols(side, c)], preferred_element_type=F32
        )

    def result_copy(i, c, kind, side, landing, peer):
        return remote(
            partial.at[kind, :, tile_cols(side, c)], landing.at[:, tile_cols(0, c)],
            r_send.at[i, c], r_recv.at[i, c], (s, peer),
        )

    results = [
        lambda c: result_copy(0, c, 0, 0, relay_a, near_1),
        lambda c: result_copy(1, c, 0, 1, relay_b, near_2),
        lambda c: result_copy(2, c, 1, 0, n1_a, near_1),
        lambda c: result_copy(3, c, 1, 1, n1_b, near_1),
        lambda c: result_copy(4, c, 2, 1, n2_b, near_2),
        lambda c: result_copy(5, c, 2, 0, n2_a, near_2),
    ]

    def send_tile(i, c, kind, side, value):
        partial[kind, :, tile_cols(side, c)] = value.astype(BF16)
        results[i](c).start()

    for kind in range(3):
        if kind > 0:
            wait_queries(kind)
        solve(kind)
        read(kind)
    w_copy.wait()
    wait_readout(0)
    for c in range(tiles):
        send_tile(0, c, 0, 0, project(0, 0, c))
        send_tile(1, c, 0, 1, project(0, 1, c))
    wait_readout(1)
    for c in range(tiles):
        send_tile(2, c, 1, 0, project(1, 0, c))
    wait_readout(2)
    for c in range(tiles):
        send_tile(4, c, 2, 1, project(2, 1, c))
    wait_queries(3)
    solve(3)
    read(3)
    for c in range(tiles):
        results[1](c).wait_recv()
        send_tile(3, c, 1, 1, project(1, 1, c) + relay_b[:, tile_cols(0, c)].astype(F32))
        results[0](c).wait_recv()
        send_tile(5, c, 2, 0, project(2, 0, c) + relay_a[:, tile_cols(0, c)].astype(F32))
    wait_readout(3)
    for c in range(tiles):
        for side in range(2):
            own[:, tile_cols(side, c)] = project(3, side, c)

    for c in range(tiles):
        for side, (i1, from_1), (i2, from_2) in (
            (0, (2, n1_a), (5, n2_a)),
            (1, (3, n1_b), (4, n2_b)),
        ):
            results[i1](c).wait_recv()
            results[i2](c).wait_recv()
            cols = tile_cols(side, c)
            out_ref[:, cols] = (
                own[:, cols]
                + from_1[:, tile_cols(0, c)].astype(F32)
                + from_2[:, tile_cols(0, c)].astype(F32)
            ).astype(BF16)

    for result in results:
        for c in range(tiles):
            result(c).wait_send()
    for fn in pending:
        fn()


def body(planes, inner, query_rows, key_rows, value_rows, log_decay, regularizer, norm_gain, out_weight):
    ring = lax.axis_size("head")
    rows, model = query_rows.shape
    heads = regularizer.shape[0]
    tokens = rows * ring * inner
    blocks = tokens // SPAN
    half = model // 2
    piece = SPAN // planes
    vm = pltpu.VMEM
    dma = pltpu.SemaphoreType.DMA
    scratch = [
        vm((inner,) + log_decay.shape, F32),
        pltpu.SMEM(regularizer.shape, F32),
        vm(norm_gain.shape, F32),
        vm((tokens, SPAN), BF16),
        vm((tokens, SPAN), BF16),
        vm((tokens, SPAN), BF16),
        vm((heads * SPAN, model), BF16),
        vm((blocks, SPAN, SPAN), F32),
        vm((blocks, SPAN, SPAN), F32),
        vm((blocks, SPAN, SPAN), F32),
        vm((blocks, 8, SPAN), F32),
        vm((blocks, 8, SPAN), F32),
        vm((8, SPAN), F32),
        vm((blocks, SPAN, SPAN), BF16),
        vm((blocks, SPAN, SPAN), BF16),
        vm((blocks, SPAN, SPAN), BF16),
        vm((blocks, SPAN, SPAN), F32),
        vm((2, blocks, SPAN, SPAN), F32),
        vm((planes, 4 * piece, SPAN), BF16),
        vm((planes, 4 * piece, SPAN), BF16),
        vm((planes, 3 * piece, SPAN), BF16),
        vm((planes, 3 * piece, SPAN), BF16),
        vm((2, SPAN, SPAN), F32),
        vm((ring, inner, rows, SPAN), F32),
        vm((ring, inner - 1, rows, SPAN), BF16),
        vm((ring, rows, heads * SPAN), BF16),
        vm((rows, model), F32),
        vm((ring - 1, rows, model), BF16),
    ]
    scratch += [vm((rows, half), BF16)] * 6
    scratch += [dma((7,))] + [dma((inner,))] * 2 + [dma((3, inner * ring))] * 2
    scratch += [dma((planes,))] * 4 + [dma((ring, inner))] * 2
    scratch += [dma((6, half // TILE))] * 2
    in_hbm = pl.BlockSpec(memory_space=pltpu.HBM)
    return pl.pallas_call(
        functools.partial(kernel, planes, inner, ring),
        out_shape=jax.ShapeDtypeStruct((rows, model), BF16),
        in_specs=[in_hbm] * 7,
        out_specs=pl.BlockSpec(memory_space=pltpu.VMEM),
        scratch_shapes=scratch,
        compiler_params=pltpu.CompilerParams(
            collective_id=0, has_side_effects=True, vmem_limit_bytes=63 * 1024 * 1024
        ),
    )(query_rows, key_rows, value_rows, log_decay, regularizer, norm_gain, out_weight)


def solution(mesh):
    placed = (
        P(("seq", "head"), None),
        P(("seq", "head"), None),
        P(("seq", "head"), None),
        P("head", "seq"),
        P("head"),
        P("head", None),
        P("head", None),
    )
    inner = 8
    planes = mesh.shape["seq"] // inner
    return jax.shard_map(
        functools.partial(body, planes, inner), mesh=mesh, in_specs=placed,
        out_specs=P(("seq", "head"), None), check_vma=False,
    )
```

time: 578 us -> 79.1 us (0.14); the launches traced: 571 us -> 78.2 us
  waiting for transfers between devices: 178 us -> 0 us
  other arithmetic: 172 us -> 0 us
  blocking collectives: 133 us -> 0 us
  Pallas kernels: 0 us -> 76.3 us
  matrix products: 41.4 us -> 0 us
  local copies, waits for them, and re-layouts: 18.1 us -> 1.87 us
  between operations: 14.6 us -> 0.01 us
  starting transfers between devices: 12.6 us -> 0 us
    select_n x64 -> x0, other arithmetic: 154 us -> none  [step(): return jax.tree.map(lambda a, b: jnp.where(reached, a, b), new, before)]
    all_gather x2 -> x0, waiting for transfers between devices: 143 us -> none  [prefix(): everything = jax.tree.map(lambda part: lax.all_gather(part, axis), shard)]
    unnamed x1 -> x0, blocking collectives: 133 us -> none
    pallas_call x0 -> x1, Pallas kernels: none -> 76.3 us  [body(): pl.pallas_call(functools.partial(kernel, planes, inner, ring), out_shape=...]
    dot_general x18 -> x0, matrix products: 41.4 us -> none  [the longest x4 9.19 us: solve_block(): jnp.einsum('...cd,...jd->...cj', direction, normed_keys, precision=HIGHEST)]
    reduce_scatter x1 -> x0, waiting for transfers between devices: 28.9 us -> none  [body(): lax.psum_scatter(jnp.dot(readout_rows, out_weight, preferred_element_type...]
    all_to_all x3 -> x0, starting transfers between devices: 12.4 us -> none  [the longest x1 4.84 us: body(): lax.all_to_all(key_rows, 'head', split_axis=1, concat_axis=0, tiled=True)]
    add x7 -> x0, other arithmetic: 7.98 us -> none  [the longest x2 2.58 us: advance(): factor * memory + memory_term]
  transfers between devices with their start and end apart: 6 -> 0, of which waited for: 5 -> 0; matrix products, arithmetic and copies ran while one was open for 3% -> 0% of each run, Pallas kernels for 0% -> 0%
where the time goes in v2:
time: 79.1 us; the launch traced here: 78.2 us
  Pallas kernels  76.3 us (96%)
  local copies, waits for them, and re-layouts  1.87 us (2%)
    pallas_call x1, Pallas kernels, body(): pl.pallas_call(functools.partial(kernel, planes, inner, ring), out_shape=...  76.3 us
    unnamed x1, local copies, waits for them, and re-layouts  1.87 us

profile of v2, /device:TPU:1, one launch (start us, length us, event | category | flops | bytes accessed | tf_op | source)
XLA Modules:
  0.0 78.2 jit_solution(13269594422613924632)
XLA Ops:
  0.0 76.3 %shard_map.73 = bf16[64,4096]{1,0:T(8,128)(2,1)} custom-call(bf16[64,4096]{1,0:T(8,128)(2,1)} %q_hbm.1, bf16[64,4096]{1,0:T(8,128)(2,1)} %k_hbm.1, bf16[64,4096]{1,0:T(8,128)(2,1)} %v_hbm.1, f32[8,256]{1,0:T(8,128)} %ld_hbm.1, f32[8]{0:T(128)} %reg_hbm.1, f32[8,128]{1,0:T(8,128)} %gain_hbm.1, bf16[1024,4096]{1,0:T(8,128)(2,1)} %w_hbm.1), custom_call_target="tpu_custom_call" | custom-call | tf_op jit(solution)/shard_map/pallas_call | solution.py:560
  76.3 1.9 %copy.9 = bf16[64,4096]{1,0:T(8,128)(2,1)} copy(bf16[64,4096]{1,0:T(8,128)(2,1)} %shard_map.73) | data formatting | bytes 1048576

commit v3 on v2

--- a/solution.py
+++ b/solution.py
@@ -24,7 +24,7 @@
     planes, inner, ring,
     q_hbm, k_hbm, v_hbm, ld_hbm, reg_hbm, gain_hbm, w_hbm, out_ref,
     ld_plane, reg_ref, gain_ref, qb, kb, vb, wv, weights, carried, tails, leave, enter, dec_total,
-    knorm, klow, tailed, terms, before, z_to, z_in, z_out, z_back, z_state,
+    kpair, tailed, terms, before, z_to, z_in, z_out, z_back, z_state,
     solved, sending, readout, own, partial,
     relay_a, relay_b, n1_a, n1_b, n2_a, n2_b,
     local_sem, ld_send, ld_recv, g_send, g_recv,
@@ -35,7 +35,7 @@
     z = lax.div(s, inner)
     me = lax.rem(s, inner)
     rows = q_hbm.shape[0]
-    blocks = knorm.shape[0]
+    blocks = kpair.shape[0]
     per_device = blocks // inner
     half = w_hbm.shape[1] // 2
     pending = []
@@ -198,27 +198,43 @@
     def plane_states(t):
         mine, ((_, got),) = got_group[t]
 
-        def states(over):
-            source = lax.rem(me + inner - over, inner)
-            for n in range(per_device):
-                b = source * per_device + n
-                if t == 0:
-                    key = kb[block_rows(b), :].astype(F32)
-                    square = jnp.mean(key * key, axis=-1, keepdims=True)
-                    normed = key * (lax.rsqrt(square + EPSILON) * SPAN ** -0.5)
-                    right, right_low = split(normed)
-                    knorm[b] = right
-                    klow[b] = right_low
-                    left, left_low = split(tails[b] * normed)
-                    tailed[b] = left
-                    left = jnp.concatenate([left, left_low, left], axis=0)
-                    right = jnp.concatenate([right, right, right_low], axis=0)
-                else:
-                    right = vb[block_rows(b), :]
-                    left = tailed[b]
-                terms[b] = lax.dot_general(
-                    left, right, COLS_BY_COLS, preferred_element_type=F32
-                )
+        def states(overs):
+            bs = [
+                lax.rem(me + inner - over, inner) * per_device + n
+                for over in overs
+                for n in range(per_device)
+            ]
+            if t == 0:
+                keys = [kb[block_rows(b), :].astype(F32) for b in bs]
+                scales = [
+                    lax.rsqrt(jnp.mean(key * key, axis=-1, keepdims=True) + EPSILON)
+                    * SPAN ** -0.5
+                    for key in keys
+                ]
+                normed = [key * scale for key, scale in zip(keys, scales)]
+                pairs = [split(value) for value in normed]
+                lefts = [split(tails[b] * value) for b, value in zip(bs, normed)]
+                products = [
+                    lax.dot_general(
+                        jnp.concatenate([left[0], left[1], left[0]], axis=0),
+                        jnp.concatenate([pair[0], pair[0], pair[1]], axis=0),
+                        COLS_BY_COLS, preferred_element_type=F32,
+                    )
+                    for left, pair in zip(lefts, pairs)
+                ]
+                for b, pair, left in zip(bs, pairs, lefts):
+                    kpair[b, :SPAN, :], kpair[b, SPAN:, :] = pair
+                    tailed[b] = left[0]
+            else:
+                products = [
+                    lax.dot_general(
+                        tailed[b], vb[block_rows(b), :], COLS_BY_COLS,
+                        preferred_element_type=F32,
+                    )
+                    for b in bs
+                ]
+            for b, product in zip(bs, products):
+                terms[b] = product
 
         def batch(i):
             if isinstance(i, int):
@@ -226,8 +242,7 @@
                 loop(1, BATCH * ring, got)
             else:
                 loop(i * BATCH * ring, (i + 1) * BATCH * ring, got)
-            for n in range(BATCH):
-                states(i * BATCH + n)
+            states([i * BATCH + n for n in range(BATCH)])
 
         batch(0)
         loop(1, inner // BATCH, batch)
@@ -332,12 +347,16 @@
         )
 
     def correlate(vector, b):
-        high, low = split(vector)
-        key = knorm[b]
-        return lax.dot_general(
-            jnp.concatenate([high, low], axis=1), jnp.concatenate([key, key], axis=1),
-            ROWS_BY_ROWS, preferred_element_type=F32,
-        ) + lax.dot_general(high, klow[b], ROWS_BY_ROWS, preferred_element_type=F32)
+        return add_terms(
+            lax.dot_general(
+                jnp.concatenate(split(vector), axis=0), kpair[b], ROWS_BY_ROWS,
+                preferred_element_type=F32,
+            )
+        )
+
+    def add_terms(products):
+        high, low = products[:rows, :], products[rows:, :]
+        return high[:, :SPAN] + (high[:, SPAN:] + low[:, :SPAN])
 
     def solve(kind):
         each = range(inner)
@@ -346,10 +365,15 @@
         ridge = reg_ref[me]
         states = [split(start_state(0, b)) for b in bs]
         mixed = [
-            jnp.concatenate([states[i][0], knorm[bs[i]], states[i][0], knorm[bs[i]]], axis=0)
+            jnp.concatenate(
+                [
+                    jnp.concatenate(states[i], axis=1),
+                    jnp.concatenate([kpair[bs[i], :SPAN, :], kpair[bs[i], SPAN:, :]], axis=1),
+                ],
+                axis=0,
+            )
             for i in each
         ]
-        mixed_low = [jnp.concatenate([states[i][1], klow[bs[i]]], axis=0) for i in each]
         direction = [qb[slot((member(i), chunks[kind])), :].astype(F32) for i in each]
         residual = list(direction)
         answer = [None] * inner
@@ -358,16 +382,18 @@
             corr = [correlate(direction[i], bs[i]) for i in each]
             from_state = [split(carried[bs[i], here, :] * direction[i]) for i in each]
             from_block = [split(corr[i] * weights[bs[i], here, :]) for i in each]
-            high = [
-                jnp.concatenate([from_state[i][0], from_block[i][0]], axis=1) for i in each
-            ]
             both = [
-                jnp.concatenate([high[i], from_state[i][1], from_block[i][1]], axis=1)
+                jnp.concatenate(
+                    [
+                        jnp.concatenate([from_state[i][n], from_block[i][n]], axis=1)
+                        for n in range(2)
+                    ],
+                    axis=0,
+                )
                 for i in each
             ]
             mapped = [
-                jnp.dot(both[i], mixed[i], preferred_element_type=F32)
-                + jnp.dot(high[i], mixed_low[i], preferred_element_type=F32)
+                add_terms(jnp.dot(both[i], mixed[i], preferred_element_type=F32))
                 + ridge * direction[i]
                 for i in each
             ]
@@ -396,37 +422,49 @@
     def read(kind):
         gain = pick_row(gain_ref[...], me)
         here = token_rows(kind)
-        for i in range(inner):
-            o = i + 1
-            b = block_of(kind, i)
-            answer = solved[kind, i]
-            corr = correlate(answer, b)
-            left = jnp.concatenate(
+        each = range(inner)
+        bs = [block_of(kind, i) for i in each]
+        answers = [solved[kind, i] for i in each]
+        corr = [correlate(answers[i], bs[i]) for i in each]
+        left = [
+            jnp.concatenate(
                 [
-                    (carried[b, here, :] * answer).astype(BF16),
-                    (corr * weights[b, here, :]).astype(BF16),
+                    (carried[bs[i], here, :] * answers[i]).astype(BF16),
+                    (corr[i] * weights[bs[i], here, :]).astype(BF16),
                 ],
                 axis=1,
             )
-            mixed = jnp.concatenate([start_state(1, b).astype(BF16), vb[block_rows(b), :]], axis=0)
-            raw = jnp.dot(left, mixed, preferred_element_type=F32)
-            scale = lax.rsqrt(jnp.mean(raw * raw, axis=-1, keepdims=True) + EPSILON)
-            normed = (raw * scale * gain).astype(BF16)
+            for i in each
+        ]
+        mixed = [
+            jnp.concatenate([start_state(1, b).astype(BF16), vb[block_rows(b), :]], axis=0)
+            for b in bs
+        ]
+        raws = [jnp.dot(left[i], mixed[i], preferred_element_type=F32) for i in each]
+        scales = [
+            lax.rsqrt(jnp.mean(raw * raw, axis=-1, keepdims=True) + EPSILON) for raw in raws
+        ]
+        results_of = [(raws[i] * scales[i] * gain).astype(BF16) for i in each]
+        for i in each:
+            o = i + 1
+            normed = results_of[i]
             if o == inner:
                 readout[kind, :, state_cols(me)] = normed
             else:
                 sending[kind, i] = normed
-                copy = remote(
-                    sending.at[kind, i], readout.at[kind, :, state_cols(me)],
-                    b_send.at[kind, o], b_recv.at[kind, o], plane[3](shift_plane(o, 1)),
-                )
-                copy.start()
-                pending.append(copy.wait_send)
-                back = shift_plane(o, -1)
-                b_done[kind, o] = remote(
-                    sending.at[kind, i], readout.at[kind, :, state_cols(back)],
-                    b_send.at[kind, o], b_recv.at[kind, o], plane[3](back),
-                ).wait_recv
+        for i in range(inner - 1):
+            o = i + 1
+            copy = remote(
+                sending.at[kind, i], readout.at[kind, :, state_cols(me)],
+                b_send.at[kind, o], b_recv.at[kind, o], plane[3](shift_plane(o, 1)),
+            )
+            copy.start()
+            pending.append(copy.wait_send)
+            back = shift_plane(o, -1)
+            b_done[kind, o] = remote(
+                sending.at[kind, i], readout.at[kind, :, state_cols(back)],
+                b_send.at[kind, o], b_recv.at[kind, o], plane[3](back),
+            ).wait_recv
 
     def wait_readout(kind):
         for o in range(1, inner):
@@ -458,9 +496,14 @@
         lambda c: result_copy(5, c, 2, 0, n2_a, near_2),
     ]
 
-    def send_tile(i, c, kind, side, value):
-        partial[kind, :, tile_cols(side, c)] = value.astype(BF16)
-        results[i](c).start()
+    def send_tiles(cs, batch):
+        for c in cs:
+            values = [project(kind, side, c) for _, kind, side in batch]
+            for (_, kind, side), value in zip(batch, values):
+                partial[kind, :, tile_cols(side, c)] = value.astype(BF16)
+        for c in cs:
+            for i, _, _ in batch:
+                results[i](c).start()
 
     for kind in range(3):
         if kind > 0:
@@ -469,23 +512,28 @@
         read(kind)
     w_copy.wait()
     wait_readout(0)
-    for c in range(tiles):
-        send_tile(0, c, 0, 0, project(0, 0, c))
-        send_tile(1, c, 0, 1, project(0, 1, c))
+    for c in range(0, tiles, 2):
+        send_tiles((c, c + 1), ((0, 0, 0), (1, 0, 1)))
     wait_readout(1)
-    for c in range(tiles):
-        send_tile(2, c, 1, 0, project(1, 0, c))
+    send_tiles(range(tiles), ((2, 1, 0),))
     wait_readout(2)
-    for c in range(tiles):
-        send_tile(4, c, 2, 1, project(2, 1, c))
+    send_tiles(range(tiles), ((4, 2, 1),))
     wait_queries(3)
     solve(3)
     read(3)
     for c in range(tiles):
+        here = tile_cols(0, c)
+        values = project(1, 1, c), project(2, 0, c)
+        own[:, here], own[:, tile_cols(1, c)] = values
+    for c in range(tiles):
         results[1](c).wait_recv()
-        send_tile(3, c, 1, 1, project(1, 1, c) + relay_b[:, tile_cols(0, c)].astype(F32))
         results[0](c).wait_recv()
-        send_tile(5, c, 2, 0, project(2, 0, c) + relay_a[:, tile_cols(0, c)].astype(F32))
+        here = tile_cols(0, c)
+        there = tile_cols(1, c)
+        partial[1, :, there] = (own[:, here] + relay_b[:, here].astype(F32)).astype(BF16)
+        partial[2, :, here] = (own[:, there] + relay_a[:, here].astype(F32)).astype(BF16)
+        results[3](c).start()
+        results[5](c).start()
     wait_readout(3)
     for c in range(tiles):
         for side in range(2):
@@ -536,8 +584,7 @@
         vm((blocks, 8, SPAN), F32),
         vm((blocks, 8, SPAN), F32),
         vm((8, SPAN), F32),
-        vm((blocks, SPAN, SPAN), BF16),
-        vm((blocks, SPAN, SPAN), BF16),
+        vm((blocks, 2 * SPAN, SPAN), BF16),
         vm((blocks, SPAN, SPAN), BF16),
         vm((blocks, SPAN, SPAN), F32),
         vm((2, blocks, SPAN, SPAN), F32),
@@ -559,12 +606,12 @@
     in_hbm = pl.BlockSpec(memory_space=pltpu.HBM)
     return pl.pallas_call(
         functools.partial(kernel, planes, inner, ring),
-        out_shape=jax.ShapeDtypeStruct((rows, model), BF16),
+        out_shape=pltpu.VMEM((rows, model), BF16),
         in_specs=[in_hbm] * 7,
         out_specs=pl.BlockSpec(memory_space=pltpu.VMEM),
         scratch_shapes=scratch,
         compiler_params=pltpu.CompilerParams(
-            collective_id=0, has_side_effects=True, vmem_limit_bytes=63 * 1024 * 1024
+            collective_id=0, has_side_effects=True, vmem_limit_bytes=60 * 1024 * 1024
         ),
     )(query_rows, key_rows, value_rows, log_decay, regularizer, norm_gain, out_weight)
 

time: 79.1 us -> 67.9 us (0.86); the launches traced: 78.2 us -> 67.8 us
  Pallas kernels: 76.3 us -> 67 us
  local copies, waits for them, and re-layouts: 1.87 us -> 0.8 us
    pallas_call x1, Pallas kernels: 76.3 us -> 67 us  [body(): pl.pallas_call(functools.partial(kernel, planes, inner, ring), out_shape=...]
    unnamed x1, local copies, waits for them, and re-layouts: 1.87 us -> 0.8 us
where the time goes in v3:
time: 67.9 us; the launch traced here: 67.8 us
  Pallas kernels  67 us (99%)
  local copies, waits for them, and re-layouts  0.8 us (1%)
    pallas_call x1, Pallas kernels, body(): pl.pallas_call(functools.partial(kernel, planes, inner, ring), out_shape=...  67 us

profile of v3, /device:TPU:1, one launch (start us, length us, event | category | flops | bytes accessed | tf_op | source)
XLA Modules:
  0.0 67.8 jit_solution(10068867569733302095)
XLA Ops:
  0.0 67.0 %shard_map.73 = bf16[64,4096]{1,0:T(8,128)(2,1)S(1)} custom-call(bf16[64,4096]{1,0:T(8,128)(2,1)} %q_hbm.1, bf16[64,4096]{1,0:T(8,128)(2,1)} %k_hbm.1, bf16[64,4096]{1,0:T(8,128)(2,1)} %v_hbm.1, f32[8,256]{1,0:T(8,128)} %ld_hbm.1, f32[8]{0:T(128)} %reg_hbm.1, f32[8,128]{1,0:T(8,128)} %gain_hbm.1, bf16[1024,4096]{1,0:T(8,128)(2,1)} %w_hbm.1), custom_call_target="tpu_custom_call" | custom-call | tf_op jit(solution)/shard_map/pallas_call | solution.py:607
  67.0 0.8 %copy.9 = bf16[64,4096]{1,0:T(8,128)(2,1)} copy(bf16[64,4096]{1,0:T(8,128)(2,1)S(1)} %shard_map.73) | data formatting | bytes 1048576

commit v4 on v3

--- a/solution.py
+++ b/solution.py
@@ -23,7 +23,7 @@
 def kernel(
     planes, inner, ring,
     q_hbm, k_hbm, v_hbm, ld_hbm, reg_hbm, gain_hbm, w_hbm, out_ref,
-    ld_plane, reg_ref, gain_ref, qb, kb, vb, wv, weights, carried, tails, leave, enter, dec_total,
+    ld_plane, reg_ref, gain_ref, qb, kb, vb, wv, weights, carried, tails, leave, enter, to_end, dec_total,
     kpair, tailed, terms, before, z_to, z_in, z_out, z_back, z_state,
     solved, sending, readout, own, partial,
     relay_a, relay_b, n1_a, n1_b, n2_a, n2_b,
@@ -87,7 +87,8 @@
         pending.append(lambda: loop(first, count, lambda o: copy(o, 1).wait_send()))
         if later:
             return (lambda o: copy(o, 1).start()), (lambda o: copy(o, -1).wait_recv())
-        loop(first, count, lambda o: copy(o, 1).start())
+        for o in range(first, count):
+            copy(o, 1).start()
         return lambda o: copy(o, -1).wait_recv()
 
     def all_of(partners, got):
@@ -181,12 +182,15 @@
         last = jnp.broadcast_to(row[:, SPAN - 1:SPAN], (8, SPAN))
         enter[b] = jnp.exp(total)
         total = total + last
+        to_end[b] = total
         cum = down(row)
         tails[b] = jnp.exp(last[0:1, :] - cum)
         weights[b] = jnp.where(causal, jnp.exp(jnp.minimum(cum - row, 0.0)), 0.0)
         carried[b] = jnp.exp(cum)
         leave[b] = jnp.exp(last)
     dec_total[...] = total
+    for b in range(blocks):
+        to_end[b] = jnp.exp(total - to_end[b])
 
     def split(value):
         high = value.astype(BF16)
@@ -198,7 +202,7 @@
     def plane_states(t):
         mine, ((_, got),) = got_group[t]
 
-        def states(overs):
+        def states(overs, acc):
             bs = [
                 lax.rem(me + inner - over, inner) * per_device + n
                 for over in overs
@@ -235,21 +239,18 @@
                 ]
             for b, product in zip(bs, products):
                 terms[b] = product
-
-        def batch(i):
-            if isinstance(i, int):
-                mine.wait()
-                loop(1, BATCH * ring, got)
-            else:
-                loop(i * BATCH * ring, (i + 1) * BATCH * ring, got)
-            states([i * BATCH + n for n in range(BATCH)])
-
-        batch(0)
-        loop(1, inner // BATCH, batch)
-        plane_total = jnp.zeros((SPAN, SPAN), F32)
-        for b in range(blocks):
-            before[t, b] = plane_total
-            plane_total = leave[b][0:1, :] * plane_total + terms[b]
+                acc = acc + to_end[b][0:1, :] * product
+            return acc
+
+        mine.wait()
+        loop(1, BATCH * ring, got)
+        plane_total = states(list(range(BATCH)), jnp.zeros((SPAN, SPAN), F32))
+
+        def batch(i, acc):
+            loop(i * BATCH * ring, (i + 1) * BATCH * ring, got)
+            return states([i * BATCH + n for n in range(BATCH)], acc)
+
+        plane_total = lax.fori_loop(1, inner // BATCH, batch, plane_total)
         for i in range(planes):
             rows_of = plane_total[i * piece:(i + 1) * piece, :]
             if t == 0:
@@ -257,9 +258,18 @@
             else:
                 z_to[i, 2 * piece:3 * piece, :] = rows_of.astype(BF16)
 
+    def block_starts(t):
+        acc = jnp.zeros((SPAN, SPAN), F32)
+        for b in range(0, blocks, 2):
+            factors = leave[b][0:1, :], leave[b + 1][0:1, :]
+            added = terms[b], terms[b + 1]
+            middle = factors[0] * acc + added[0]
+            before[t, b], before[t, b + 1] = acc, middle
+            acc = factors[1] * middle + added[1]
+
     piece = SPAN // planes
 
-    def send_z():
+    def pack_decay():
         rest = dec_total[0:1, :]
         terms_of = []
         for _ in range(3):
@@ -273,6 +283,8 @@
         packed = packed.astype(BF16)
         for i in range(planes):
             z_to[i, 3 * piece:4 * piece, :] = packed
+
+    def send_z():
         got = exchange(
             column, lambda to, frm: (z_to.at[to], z_in.at[frm]),
             lambda o: z_send.at[o], lambda o: z_recv.at[o], z,
@@ -281,17 +293,17 @@
         return got
 
     def z_prefix():
-        gram = jnp.zeros((piece, SPAN), F32)
-        memory = gram
+        arrived = [z_in[i].astype(F32) for i in range(planes - 1)]
+        tails_in = [part[3 * piece:4 * piece, :] for part in arrived]
+        decays = [jnp.exp(tail[0:1, :] + tail[1:2, :] + tail[2:3, :]) for tail in tails_in]
+        grams = [jnp.zeros((piece, SPAN), F32)]
+        memories = [grams[0]]
+        for part, decay in zip(arrived, decays):
+            grams.append(decay * grams[-1] + (part[0:piece, :] + part[piece:2 * piece, :]))
+            memories.append(decay * memories[-1] + part[2 * piece:3 * piece, :])
         for i in range(planes):
-            z_out[i, 0:piece, :], z_out[i, piece:2 * piece, :] = split(gram)
-            z_out[i, 2 * piece:3 * piece, :] = memory.astype(BF16)
-            if i + 1 < planes:
-                arrived = z_in[i].astype(F32)
-                tail = arrived[3 * piece:4 * piece, :]
-                decay = jnp.exp(tail[0:1, :] + tail[1:2, :] + tail[2:3, :])
-                gram = decay * gram + (arrived[0:piece, :] + arrived[piece:2 * piece, :])
-                memory = decay * memory + arrived[2 * piece:3 * piece, :]
+            z_out[i, 0:piece, :], z_out[i, piece:2 * piece, :] = split(grams[i])
+            z_out[i, 2 * piece:3 * piece, :] = memories[i].astype(BF16)
 
     def send_z_back():
         got = exchange(
@@ -302,11 +314,11 @@
         return got
 
     def collect():
+        arrived = [z_back[i].astype(F32) for i in range(planes)]
         for i in range(planes):
-            arrived = z_back[i].astype(F32)
             here = slice(i * piece, (i + 1) * piece)
-            z_state[0, here, :] = arrived[0:piece, :] + arrived[piece:2 * piece, :]
-            z_state[1, here, :] = arrived[2 * piece:3 * piece, :]
+            z_state[0, here, :] = arrived[i][0:piece, :] + arrived[i][piece:2 * piece, :]
+            z_state[1, here, :] = arrived[i][2 * piece:3 * piece, :]
 
     def wait_queries(kind):
         mine, moves = got_group[2]
@@ -314,14 +326,19 @@
             mine.wait()
         all_of(kinds[kind], moves[kind][1])
 
+    pack_decay()
     plane_states(0)
+    block_starts(0)
     plane_states(1)
     got_z = send_z()
-    for kind in range(4):
-        go_group(2, kind)
+    go_group(2, 0)
+    go_group(2, 1)
+    block_starts(1)
     all_of(column, got_z)
     z_prefix()
     got_zb = send_z_back()
+    go_group(2, 2)
+    go_group(2, 3)
     w_copy.start()
     wait_queries(0)
     all_of(column, got_zb)
@@ -583,6 +600,7 @@
         vm((blocks, SPAN, SPAN), F32),
         vm((blocks, 8, SPAN), F32),
         vm((blocks, 8, SPAN), F32),
+        vm((blocks, 8, SPAN), F32),
         vm((8, SPAN), F32),
         vm((blocks, 2 * SPAN, SPAN), BF16),
         vm((blocks, SPAN, SPAN), BF16),

time: 67.9 us -> 67.8 us (level)
  no operation moved by 1% of the time
where the time goes in v4:
time: 67.8 us; the launch traced here: 67.7 us
  Pallas kernels  66.9 us (99%)
  local copies, waits for them, and re-layouts  0.8 us (1%)
    pallas_call x1, Pallas kernels, body(): pl.pallas_call(functools.partial(kernel, planes, inner, ring), out_shape=...  66.9 us

profile of v4, /device:TPU:1, one launch (start us, length us, event | category | flops | bytes accessed | tf_op | source)
XLA Modules:
  0.0 67.7 jit_solution(5985944504458923835)
XLA Ops:
  0.0 66.9 %shard_map.73 = bf16[64,4096]{1,0:T(8,128)(2,1)S(1)} custom-call(bf16[64,4096]{1,0:T(8,128)(2,1)} %q_hbm.1, bf16[64,4096]{1,0:T(8,128)(2,1)} %k_hbm.1, bf16[64,4096]{1,0:T(8,128)(2,1)} %v_hbm.1, f32[8,256]{1,0:T(8,128)} %ld_hbm.1, f32[8]{0:T(128)} %reg_hbm.1, f32[8,128]{1,0:T(8,128)} %gain_hbm.1, bf16[1024,4096]{1,0:T(8,128)(2,1)} %w_hbm.1), custom_call_target="tpu_custom_call" | custom-call | tf_op jit(solution)/shard_map/pallas_call | solution.py:625
  66.9 0.8 %copy.9 = bf16[64,4096]{1,0:T(8,128)(2,1)} copy(bf16[64,4096]{1,0:T(8,128)(2,1)S(1)} %shard_map.73) | data formatting | bytes 1048576

commit v5 on v4

--- a/solution.py
+++ b/solution.py
@@ -11,7 +11,7 @@
 ITERS = 4
 EPSILON = 1e-06
 TILE = 512
-BATCH = 2
+BATCH = 1
 MESH = pl.DeviceIdType.MESH
 HIGHEST = lax.Precision.HIGHEST
 F32 = jnp.float32

time: 67.8 us -> 70.9 us (1.046)
  Pallas kernels: 66.9 us -> 70 us
    pallas_call x1, Pallas kernels: 66.9 us -> 70 us  [body(): pl.pallas_call(functools.partial(kernel, planes, inner, ring), out_shape=...]
where the time goes in v5:
time: 70.9 us; the launch traced here: 70.8 us
  Pallas kernels  70 us (99%)
  local copies, waits for them, and re-layouts  0.8 us (1%)
    pallas_call x1, Pallas kernels, body(): pl.pallas_call(functools.partial(kernel, planes, inner, ring), out_shape=...  70 us

profile of v5, /device:TPU:1, one launch (start us, length us, event | category | flops | bytes accessed | tf_op | source)
XLA Modules:
  0.0 70.8 jit_solution(14507434829493371960)
XLA Ops:
  0.0 70.0 %shard_map.73 = bf16[64,4096]{1,0:T(8,128)(2,1)S(1)} custom-call(bf16[64,4096]{1,0:T(8,128)(2,1)} %q_hbm.1, bf16[64,4096]{1,0:T(8,128)(2,1)} %k_hbm.1, bf16[64,4096]{1,0:T(8,128)(2,1)} %v_hbm.1, f32[8,256]{1,0:T(8,128)} %ld_hbm.1, f32[8]{0:T(128)} %reg_hbm.1, f32[8,128]{1,0:T(8,128)} %gain_hbm.1, bf16[1024,4096]{1,0:T(8,128)(2,1)} %w_hbm.1), custom_call_target="tpu_custom_call" | custom-call | tf_op jit(solution)/shard_map/pallas_call | solution.py:625
  70.0 0.8 %copy.9 = bf16[64,4096]{1,0:T(8,128)(2,1)} copy(bf16[64,4096]{1,0:T(8,128)(2,1)S(1)} %shard_map.73) | data formatting | bytes 1048576
